TPU v7x, 32 devices: a whole 2x2x4 slice. The times are simulated.
32 devices in a mesh: kv: 4 (over x, core), seq: 8 (over z, y).
Axes of the slice: x: 2, y: 2, z: 4, core: 2. Of those that a mesh axis runs over, the one named last changes fastest.
Arguments:
- hidden_states: bfloat16 [1536, 2048], P('seq')
- attn_gain: float32 [2048], replicated, may hold values from 0.5 to 1.5
- w_q: bfloat16 [2048, 2048], P(None, 'kv')
- w_k: bfloat16 [2048, 512], P(None, 'kv')
- w_v: bfloat16 [2048, 512], P(None, 'kv'), may hold values from -0.125 to 0.125
- w_o: bfloat16 [2048, 2048], P('kv'), may hold values from -0.125 to 0.125
- final_gain: float32 [2048], replicated, may hold values from 0.5 to 1.5
- w_head: bfloat16 [2048, 49408], P(None, ('kv', 'seq'))
- doc_lengths: int32 [8], replicated, may hold values from 1 to 768, as said below
- target_ids: int32 [1536], replicated, may hold values from 0 to 49154, as said below
- vocab_mask: int32 [49408], P(('kv', 'seq')), may hold values from 0 to 1, as said below
Outputs:
- log_probs: float32 [1536], P('seq')
- entropies: float32 [1536], P('seq')
Inputs may be any that keep to these rules, and one draw needn't show every extreme that they name: `doc_lengths`: they sum to 1536; one is 768, one more is over 384, every other is under 64. `target_ids`: each names an entry whose vocab_mask is 1. `vocab_mask`: entries from 49155 on are 0.
All inputs are finite; a program needn't handle non-finite values.
Results may differ from a plain program's by a relative error of at most 0.0045.
Values may be sent and summed in bfloat16 or wider, within the bound.
A program may use at most 128 MiB of HBM per device.

v0:
```python
import math

import jax
import jax.numpy as jnp
from jax import lax
from jax.sharding import PartitionSpec as P

HEAD_DIM = 64


ROPE_THETA = 10000000.0
NORM_EPS = 1e-05
NEG_FILL = -1e30
ATTN_SCALE = 0.015625
RESID_SCALE = 5.0
LOGIT_SCALE = 0.125


def rms_norm(values, gain_vec):
    return (
        values * lax.rsqrt(jnp.mean(values * values, axis=-1, keepdims=True) + NORM_EPS) * gain_vec
    )


def rotate(values, positions):
    half_dim = values.shape[-1] // 2
    inverse = jnp.exp(
        jnp.arange(half_dim, dtype=jnp.float32) * (-2.0 * math.log(ROPE_THETA) / values.shape[-1])
    )
    angles = positions.astype(jnp.float32)[:, None] * inverse[None, :]
    cos_val = jnp.cos(angles)[:, None, :]
    sine_val = jnp.sin(angles)[:, None, :]
    lower_half = values[..., :half_dim]
    upper_half = values[..., half_dim:]
    return jnp.concatenate(
        [
            lower_half * cos_val - upper_half * sine_val,
            upper_half * cos_val + lower_half * sine_val,
        ],
        axis=-1,
    )


def local(
    hidden_states,
    attn_gain,
    w_q,
    w_k,
    w_v,
    w_o,
    final_gain,
    w_head,
    doc_lengths,
    target_ids,
    vocab_mask,
):
    tok_rows = hidden_states.shape[0]
    seq_index = lax.axis_index("seq")
    kv_local = w_k.shape[1] // HEAD_DIM
    q_local = w_q.shape[1] // HEAD_DIM
    group_size = q_local // kv_local
    key_width = kv_local * HEAD_DIM
    stream = hidden_states.astype(jnp.float32)
    normed_in = rms_norm(stream, attn_gain).astype(jnp.bfloat16)
    queries = jnp.dot(normed_in, w_q, preferred_element_type=jnp.float32)
    key_proj = jnp.dot(normed_in, w_k, preferred_element_type=jnp.float32)
    value_proj = jnp.dot(normed_in, w_v, preferred_element_type=jnp.float32)
    token_pos = seq_index * tok_rows + jnp.arange(tok_rows, dtype=jnp.int32)
    doc_ends = jnp.cumsum(doc_lengths)
    doc_starts = doc_ends - doc_lengths
    doc_start = jnp.max(
        jnp.where(doc_starts[None, :] <= token_pos[:, None], doc_starts[None, :], 0), axis=1
    )
    positions = token_pos - doc_start
    rotated_q = rotate(queries.reshape(tok_rows, q_local, HEAD_DIM), positions).astype(jnp.bfloat16)
    rotated_q = rotated_q.reshape(tok_rows, kv_local, group_size, HEAD_DIM)
    rotated_k = rotate(key_proj.reshape(tok_rows, kv_local, HEAD_DIM), positions).astype(
        jnp.bfloat16
    )
    packed = jnp.concatenate(
        [rotated_k.reshape(tok_rows, key_width), value_proj.astype(jnp.bfloat16)], axis=1
    )
    earliest = doc_start[0]
    latest = token_pos[tok_rows - 1]
    initial = (
        jnp.full((kv_local, group_size, tok_rows), NEG_FILL, jnp.float32),
        jnp.zeros((kv_local, group_size, tok_rows), jnp.float32),
        jnp.zeros((kv_local, group_size, tok_rows, HEAD_DIM), jnp.float32),
    )
    shard_rows = lax.all_gather(packed, "seq", axis=0, tiled=True)
    offset = jnp.int32(0)
    row_count = shard_rows.shape[0]
    key_pos = jnp.arange(row_count, dtype=jnp.int32)

    def update(current):
        top_score, totals, context_sum = current
        key_rows = shard_rows[:, :key_width].reshape(row_count, kv_local, HEAD_DIM)
        value_rows = shard_rows[:, key_width:].reshape(row_count, kv_local, HEAD_DIM)
        scores = (
            jnp.einsum("tkgd,skd->kgts", rotated_q, key_rows, preferred_element_type=jnp.float32)
            * ATTN_SCALE
        )
        allowed = (key_pos[None, :] >= doc_start[:, None]) & (
            key_pos[None, :] <= token_pos[:, None]
        )
        scores = jnp.where(allowed, scores, NEG_FILL)
        new_top = jnp.maximum(top_score, jnp.max(scores, axis=-1))
        weights = jnp.where(allowed, jnp.exp(scores - new_top[..., None]), 0.0)
        rescale = jnp.exp(top_score - new_top)
        totals = jnp.sum(weights, axis=-1)
        context_sum = jnp.einsum(
            "kgts,skd->kgtd",
            weights.astype(jnp.bfloat16),
            value_rows,
            preferred_element_type=jnp.float32,
        )
        return (new_top, totals, context_sum)

    skip_piece = (offset + row_count <= earliest) | (offset > latest)
    top_score, totals, context_sum = lax.cond(skip_piece, lambda current: current, update, initial)
    context = (
        (context_sum / totals[..., None])
        .transpose(2, 0, 1, 3)
        .reshape(tok_rows, q_local * HEAD_DIM)
        .astype(jnp.bfloat16)
    )
    vocab_local = w_head.shape[1]
    flat_rank = lax.axis_index(("kv", "seq"))
    live_mask = vocab_mask == 1
    columns = flat_rank * vocab_local + jnp.arange(vocab_local, dtype=jnp.int32)
    attn_out = lax.psum(jnp.dot(context, w_o, preferred_element_type=jnp.float32), "kv")
    final_in = rms_norm(stream + RESID_SCALE * attn_out, final_gain).astype(jnp.bfloat16)
    head_shard_rows = lax.all_gather(final_in, "seq", axis=0, tiled=True)
    logits = jnp.dot(head_shard_rows, w_head, preferred_element_type=jnp.float32) * LOGIT_SCALE
    masked = jnp.where(live_mask[None, :], logits, NEG_FILL)
    top_row = jnp.max(masked, axis=1)
    shifted = jnp.where(live_mask[None, :], masked - top_row[:, None], 0.0)
    expw = jnp.where(live_mask[None, :], jnp.exp(shifted), 0.0)
    target = jnp.sum(jnp.where(target_ids[:, None] == columns[None, :], logits, 0.0), axis=1)
    row_stats = jnp.stack([top_row, jnp.sum(expw, axis=1), jnp.sum(expw * shifted, axis=1), target])
    top_all = lax.pmax(row_stats[0], ("kv", "seq"))
    rescale = jnp.exp(row_stats[0] - top_all)
    total_all, spread_all, target_all = lax.psum(
        (
            row_stats[1] * rescale,
            rescale * (row_stats[2] + (row_stats[0] - top_all) * row_stats[1]),
            row_stats[3],
        ),
        ("kv", "seq"),
    )
    log_prob = target_all - top_all - jnp.log(total_all)
    entropy = jnp.log(total_all) - spread_all / total_all
    log_probs = lax.dynamic_slice_in_dim(log_prob, seq_index * tok_rows, tok_rows, 0)
    entropies = lax.dynamic_slice_in_dim(entropy, seq_index * tok_rows, tok_rows, 0)
    return (log_probs, entropies)


def solution(mesh):
    in_specs = (
        P("seq", None),
        P(),
        P(None, "kv"),
        P(None, "kv"),
        P(None, "kv"),
        P("kv", None),
        P(),
        P(None, ("kv", "seq")),
        P(),
        P(),
        P(("kv", "seq")),
    )
    out_specs = (P("seq"), P("seq"))
    return jax.shard_map(local, mesh=mesh, in_specs=in_specs, out_specs=out_specs, check_vma=False)
```

profile of v0, /device:TPU:0, one launch (start us, length us, event | category | flops | bytes accessed | tf_op | source)
XLA Modules:
  0.0 325.9 jit_solution(15768456096745110465)
XLA Ops:
  7.3 1.0 reduce-window.9
  8.3 0.7 bitcast_subtract_fusion
  9.5 0.6 slice.25
  10.1 1.4 fusion.10
  11.7 1.8 fusion.18
  13.7 1.7 convolution_convert_fusion
  15.4 36.0 %all_gather.6 = bf16[1536,256]{1,0:T(8,128)(2,1)} all-gather(bf16[192,256]{1,0:T(8,128)(2,1)S(1)} %pad_maximum_fusion.1), channel_id=1, replica_groups=mesh['kv'=4,'seq'=8] {'seq'}, dimensions={0}, use_global_device_ids=true | all-gather | bytes 884736 | tf_op jit(solution)/shard_map/all_gather | solution.py:90
  51.4 2.6 fusion.15
  55.5 11.2 %conditional.1 = (f32[2,4,192]{2,1,0:T(4,128)S(1)}, f32[2,4,192,64]{2,3,1,0:T(8,128)S(1)}) conditional(s32[]{:T(128)} %bitcast.9, (s32[1536]{0:T(1024)S(1)}, s32[1536]{0:T(1024)S(1)}, s32[192]{0:T(256)S(1)}, s32[192]{0:T(256)S(1)}, bf16[1536,256]{1,0:T(8,128)(2,1)}, /*index=5*/bf16[192,2,4,64]{0,3,2,1:T(8,128)(2,1)S(1)}) %tuple.16, () %tuple.17), branch_computations={%region_3.6_spmd, %region_6.7_spmd} | conditional | flops 635533824 | bytes 34063888 | solution.py:120
  55.8 2.3 copy.23
  58.1 1.2 fusion.20
  59.3 1.8 fusion
  61.1 2.6 fusion.3
  63.7 3.0 fusion.2
  66.7 1.8 fusion.21
  68.7 43.8 %all-reduce.3.cloned.1.call-done = f32[192,2048]{1,0:T(8,128)} async-done(((f32[192,2048]{1,0:T(8,128)}), f32[192,2048]{1,0:T(8,128)}) %all-reduce.3.cloned.1.call-update) | async-done | bytes 1572880 | tf_op jit(solution)/shard_map/psum | solution.py:131
  112.5 1.7 multiply_reduce_fusion.1
  114.2 2.6 multiply_convert_fusion
  116.9 99.2 %all-gather.2.cloned.1.call-done = bf16[1536,2048]{1,0:T(8,128)(2,1)} async-done(((bf16[192,2048]{1,0:T(8,128)(2,1)}), bf16[1536,2048]{1,0:T(8,128)(2,1)}) %all-gather.2.cloned.1.call-update) | async-done | bytes 6291472 | tf_op jit(solution)/shard_map/all_gather | solution.py:133
  216.1 16.0 %select_reduce_fusion.1 = (f32[1536]{0:T(1024)S(1)}, f32[1536,1544]{0,1:T(8,128)}) fusion(pred[1544]{0:T(1024)(128)(4,1)S(1)} %broadcast_compare_fusion, bf16[1536,2048]{1,0:T(8,128)(2,1)} %all-gather.2.cloned.1.call-done, bf16[2048,1544]{0,1:T(8,128)(2,1)} %param.20), kind=kOutput, calls=%fused_computation.18 | convolution fusion | flops 9721120768 | bytes 22109704 | tf_op jit(solution)/shard_map/dot_general | solution.py:134
  232.1 38.4 %pmax.7 = f32[1536]{0:T(1024)S(1)} all-reduce(f32[1536]{0:T(1024)S(1)} %get-tuple-element.61), channel_id=1, replica_groups=mesh['kv'=4,'seq'=8] {'kv','seq'}, use_global_device_ids=true, to_apply=%region_12.13 | all-reduce | flops 1536 | bytes 12288 | tf_op jit(solution)/shard_map/pmax | solution.py:141
  270.5 6.8 %multiply_reduce_fusion = (f32[1536]{0:T(1024)S(1)}, f32[1536]{0:T(1024)S(1)}, f32[1536]{0:T(1024)S(1)}) fusion(f32[1536,1544]{0,1:T(8,128)} %get-tuple-element.62, f32[1536]{0:T(1024)S(1)} %get-tuple-element.61, pred[1544]{0:T(1024)(128)(4,1)S(1)} %broadcast_compare_fusion, s32[1544]{0:T(1024)S(1)} %iota_add_fusion, s32[1536]{0:T(1024)S(1)} %copy-done.4), kind=kLoop, calls=%fused_computation.13 | loop fusion | flops 23711232 | bytes 9524776 | tf_op jit(solution)/shard_map/reduce_sum | solution.py:140
  277.3 41.1 %all-reduce = (f32[1536]{0:T(1024)S(1)}, f32[1536]{0:T(1024)S(1)}, f32[1536]{0:T(1024)S(1)}) all-reduce(f32[1536]{0:T(1024)S(1)} %get-tuple-element.43, f32[1536]{0:T(1024)S(1)} %get-tuple-element.56, f32[1536]{0:T(1024)S(1)} %get-tuple-element.55), channel_id=1, replica_groups=mesh['kv'=4,'seq'=8] {'kv','seq'}, use_global_device_ids=true, to_apply=%region_10.11 | all-reduce | flops 4608 | bytes 36864 | tf_op jit(solution)/shard_map/psum | solution.py:143
  318.4 0.7 fusion.14
  (38 shorter events, 1.8 us)
Async XLA Ops:
  7.2 59.5 %copy-start = (bf16[512,2048]{1,0:T(8,128)(2,1)S(1)}, bf16[512,2048]{1,0:T(8,128)(2,1)}, u32[]{:S(2)}) copy-start(bf16[512,2048]{1,0:T(8,128)(2,1)} %param.18) | copy-start | bytes 6291460
  7.2 44.3 %copy-start.1 = (bf16[192,2048]{1,0:T(8,128)(2,1)S(1)}, bf16[192,2048]{1,0:T(8,128)(2,1)}, u32[]{:S(2)}) copy-start(bf16[192,2048]{1,0:T(8,128)(2,1)} %param.13) | copy-start | bytes 2359300
  7.2 44.3 %copy-start.5 = (f32[2048]{0:T(1024)S(1)}, f32[2048]{0:T(1024)}, u32[]{:S(2)}) copy-start(f32[2048]{0:T(1024)} %param.14) | copy-start | bytes 24580
  7.2 105.3 %all-reduce.3.cloned.1.call-start = ((), (), s32[]{:S(2)}) async-start(), calls=%async_computation | async-start | bytes 3145728 | tf_op jit(solution)/shard_map/psum | solution.py:131
  66.6 47.6 %copy-start.2 = (f32[2048]{0:T(1024)S(1)}, f32[2048]{0:T(1024)}, u32[]{:S(2)}) copy-start(f32[2048]{0:T(1024)} %param.19) | copy-start | bytes 24580
  68.5 48.4 %copy-start.3 = (s32[1544]{0:T(1024)S(1)}, s32[1544]{0:T(1024)}, u32[]{:S(2)}) copy-start(s32[1544]{0:T(1024)} %param.23) | copy-start | bytes 18532
  68.5 147.6 %all-gather.2.cloned.1.call-start = ((), (), s32[]{:S(2)}) async-start(), calls=%async_computation.1 | async-start | bytes 7077888 | tf_op jit(solution)/shard_map/all_gather | solution.py:133
  116.9 153.6 %copy-start.4 = (s32[1536]{0:T(1024)S(1)}, s32[1536]{0:T(1024)}, u32[]{:S(2)}) copy-start(s32[1536]{0:T(1024)} %param.22) | copy-start | bytes 18436
Sparse Core Ops, SparseCore 0:
  68.6 43.8 all-reduce.2
  117.0 99.0 all-gather.1
where the time goes:
time: 326 us
  waiting for transfers between devices  143 us (44%)
  blocking collectives  116 us (36%)
  matrix products  28.2 us (9%)
  other arithmetic  18.6 us (6%)
  between operations  15.5 us (5%)
  local copies, waits for them, and re-layouts  4.72 us (1%)
    all_gather x1, waiting for transfers between devices, local(): head_shard_rows = lax.all_gather(final_in, 'seq', axis=0, tiled=True)  99.2 us
    psum x1, waiting for transfers between devices, local(): lax.psum(jnp.dot(context, w_o, preferred_element_type=jnp.float32), 'kv')  43.8 us
    psum x1, blocking collectives, local(): lax.psum((row_stats[1] * rescale, rescale * (row_stats[2] + (row_stats[0]...  41.1 us
    pmax x1, blocking collectives, local(): top_all = lax.pmax(row_stats[0], ('kv', 'seq'))  38.4 us
    all_gather x1, blocking collectives, local(): shard_rows = lax.all_gather(packed, 'seq', axis=0, tiled=True)  36 us
    dot_general x1, matrix products, local(): jnp.dot(head_shard_rows, w_head, preferred_element_type=jnp.float32)  16 us
    reduce_sum x1, other arithmetic, local(): jnp.sum(expw * shifted, axis=1)  6.81 us
  transfers between devices with their start and end apart: 2, of which 2 were waited for; matrix products, arithmetic and copies ran while one was open for 0% of the time, Pallas kernels for 0%

commit v1 on v0

--- a/solution.py
+++ b/solution.py
@@ -66,8 +66,8 @@
     key_proj = jnp.dot(normed_in, w_k, preferred_element_type=jnp.float32)
     value_proj = jnp.dot(normed_in, w_v, preferred_element_type=jnp.float32)
     token_pos = seq_index * tok_rows + jnp.arange(tok_rows, dtype=jnp.int32)
-    doc_ends = jnp.cumsum(doc_lengths)
-    doc_starts = doc_ends - doc_lengths
+    docs = jnp.arange(doc_lengths.shape[0], dtype=jnp.int32)
+    doc_starts = jnp.sum(jnp.where(docs[None, :] < docs[:, None], doc_lengths[None, :], 0), axis=1)
     doc_start = jnp.max(
         jnp.where(doc_starts[None, :] <= token_pos[:, None], doc_starts[None, :], 0), axis=1
     )

time: 326 us -> 326 us (level)
  no operation moved by 1% of the time
where the time goes in v1:
time: 326 us; the launch traced here: 325 us
  waiting for transfers between devices  143 us (44%)
  blocking collectives  116 us (36%)
  matrix products  28.2 us (9%)
  other arithmetic  17.9 us (5%)
  between operations  15.6 us (5%)
  local copies, waits for them, and re-layouts  4.72 us (1%)
    all_gather x1, waiting for transfers between devices, local(): head_shard_rows = lax.all_gather(final_in, 'seq', axis=0, tiled=True)  99.2 us
    psum x1, waiting for transfers between devices, local(): lax.psum(jnp.dot(context, w_o, preferred_element_type=jnp.float32), 'kv')  43.7 us
    psum x1, blocking collectives, local(): lax.psum((row_stats[1] * rescale, rescale * (row_stats[2] + (row_stats[0]...  41.1 us
    pmax x1, blocking collectives, local(): top_all = lax.pmax(row_stats[0], ('kv', 'seq'))  38.4 us
    all_gather x1, blocking collectives, local(): shard_rows = lax.all_gather(packed, 'seq', axis=0, tiled=True)  36 us
    dot_general x1, matrix products, local(): jnp.dot(head_shard_rows, w_head, preferred_element_type=jnp.float32)  16 us
    reduce_sum x1, other arithmetic, local(): jnp.sum(expw * shifted, axis=1)  6.8 us
  transfers between devices with their start and end apart: 2, of which 2 were waited for; matrix products, arithmetic and copies ran while one was open for 0% of the time, Pallas kernels for 0%

profile of v1, /device:TPU:0, one launch (start us, length us, event | category | flops | bytes accessed | tf_op | source)
XLA Modules:
  0.0 325.2 jit_solution(918487914452449250)
XLA Ops:
  7.3 0.9 select_reduce_fusion.3
  8.3 0.5 slice.24
  8.8 0.6 slice.25
  9.4 1.4 fusion.10
  11.0 1.8 fusion.18
  12.9 1.7 convolution_convert_fusion
  14.7 36.0 %all_gather.6 = bf16[1536,256]{1,0:T(8,128)(2,1)} all-gather(bf16[192,256]{1,0:T(8,128)(2,1)S(1)} %pad_maximum_fusion.1), channel_id=1, replica_groups=mesh['kv'=4,'seq'=8] {'seq'}, dimensions={0}, use_global_device_ids=true | all-gather | bytes 884736 | tf_op jit(solution)/shard_map/all_gather | solution.py:90
  50.7 2.6 fusion.15
  54.8 11.2 %conditional.1 = (f32[2,4,192]{2,1,0:T(4,128)S(1)}, f32[2,4,192,64]{2,3,1,0:T(8,128)S(1)}) conditional(s32[]{:T(128)} %bitcast.7, (s32[1536]{0:T(1024)S(1)}, s32[1536]{0:T(1024)S(1)}, s32[192]{0:T(256)S(1)}, s32[192]{0:T(256)S(1)}, bf16[1536,256]{1,0:T(8,128)(2,1)}, /*index=5*/bf16[192,2,4,64]{0,3,2,1:T(8,128)(2,1)S(1)}) %tuple.16, () %tuple.17), branch_computations={%region_3.6_spmd, %region_6.7_spmd} | conditional | flops 635533824 | bytes 34063888 | solution.py:120
  55.1 2.3 copy.23
  57.4 1.2 fusion.20
  58.6 1.8 fusion
  60.4 2.6 fusion.3
  63.0 3.0 fusion.2
  66.0 1.8 fusion.21
  68.0 43.7 %all-reduce.3.cloned.1.call-done = f32[192,2048]{1,0:T(8,128)} async-done(((f32[192,2048]{1,0:T(8,128)}), f32[192,2048]{1,0:T(8,128)}) %all-reduce.3.cloned.1.call-update) | async-done | bytes 1572880 | tf_op jit(solution)/shard_map/psum | solution.py:131
  111.7 1.7 multiply_reduce_fusion.1
  113.5 2.6 multiply_convert_fusion
  116.2 99.2 %all-gather.2.cloned.1.call-done = bf16[1536,2048]{1,0:T(8,128)(2,1)} async-done(((bf16[192,2048]{1,0:T(8,128)(2,1)}), bf16[1536,2048]{1,0:T(8,128)(2,1)}) %all-gather.2.cloned.1.call-update) | async-done | bytes 6291472 | tf_op jit(solution)/shard_map/all_gather | solution.py:133
  215.4 16.0 %select_reduce_fusion.1 = (f32[1536]{0:T(1024)S(1)}, f32[1536,1544]{0,1:T(8,128)}) fusion(pred[1544]{0:T(1024)(128)(4,1)S(1)} %broadcast_compare_fusion, bf16[1536,2048]{1,0:T(8,128)(2,1)} %all-gather.2.cloned.1.call-done, bf16[2048,1544]{0,1:T(8,128)(2,1)} %param.20), kind=kOutput, calls=%fused_computation.18 | convolution fusion | flops 9721120768 | bytes 22109704 | tf_op jit(solution)/shard_map/dot_general | solution.py:134
  231.3 38.4 %pmax.7 = f32[1536]{0:T(1024)S(1)} all-reduce(f32[1536]{0:T(1024)S(1)} %get-tuple-element.61), channel_id=1, replica_groups=mesh['kv'=4,'seq'=8] {'kv','seq'}, use_global_device_ids=true, to_apply=%region_12.13 | all-reduce | flops 1536 | bytes 12288 | tf_op jit(solution)/shard_map/pmax | solution.py:141
  269.7 6.8 %multiply_reduce_fusion = (f32[1536]{0:T(1024)S(1)}, f32[1536]{0:T(1024)S(1)}, f32[1536]{0:T(1024)S(1)}) fusion(f32[1536,1544]{0,1:T(8,128)} %get-tuple-element.62, f32[1536]{0:T(1024)S(1)} %get-tuple-element.61, pred[1544]{0:T(1024)(128)(4,1)S(1)} %broadcast_compare_fusion, s32[1544]{0:T(1024)S(1)} %iota_add_fusion, s32[1536]{0:T(1024)S(1)} %copy-done.4), kind=kLoop, calls=%fused_computation.13 | loop fusion | flops 23711232 | bytes 9524776 | tf_op jit(solution)/shard_map/reduce_sum | solution.py:140
  276.6 41.1 %all-reduce = (f32[1536]{0:T(1024)S(1)}, f32[1536]{0:T(1024)S(1)}, f32[1536]{0:T(1024)S(1)}) all-reduce(f32[1536]{0:T(1024)S(1)} %get-tuple-element.43, f32[1536]{0:T(1024)S(1)} %get-tuple-element.56, f32[1536]{0:T(1024)S(1)} %get-tuple-element.55), channel_id=1, replica_groups=mesh['kv'=4,'seq'=8] {'kv','seq'}, use_global_device_ids=true, to_apply=%region_10.11 | all-reduce | flops 4608 | bytes 36864 | tf_op jit(solution)/shard_map/psum | solution.py:143
  317.7 0.7 fusion.14
  (37 shorter events, 1.3 us)
Async XLA Ops:
  7.2 58.8 %copy-start = (bf16[512,2048]{1,0:T(8,128)(2,1)S(1)}, bf16[512,2048]{1,0:T(8,128)(2,1)}, u32[]{:S(2)}) copy-start(bf16[512,2048]{1,0:T(8,128)(2,1)} %param.18) | copy-start | bytes 6291460
  7.2 43.6 %copy-start.1 = (bf16[192,2048]{1,0:T(8,128)(2,1)S(1)}, bf16[192,2048]{1,0:T(8,128)(2,1)}, u32[]{:S(2)}) copy-start(bf16[192,2048]{1,0:T(8,128)(2,1)} %param.13) | copy-start | bytes 2359300
  7.2 43.5 %copy-start.5 = (f32[2048]{0:T(1024)S(1)}, f32[2048]{0:T(1024)}, u32[]{:S(2)}) copy-start(f32[2048]{0:T(1024)} %param.14) | copy-start | bytes 24580
  7.2 104.5 %all-reduce.3.cloned.1.call-start = ((), (), s32[]{:S(2)}) async-start(), calls=%async_computation | async-start | bytes 3145728 | tf_op jit(solution)/shard_map/psum | solution.py:131
  65.9 47.6 %copy-start.2 = (f32[2048]{0:T(1024)S(1)}, f32[2048]{0:T(1024)}, u32[]{:S(2)}) copy-start(f32[2048]{0:T(1024)} %param.19) | copy-start | bytes 24580
  67.8 48.4 %copy-start.3 = (s32[1544]{0:T(1024)S(1)}, s32[1544]{0:T(1024)}, u32[]{:S(2)}) copy-start(s32[1544]{0:T(1024)} %param.23) | copy-start | bytes 18532
  67.8 147.6 %all-gather.2.cloned.1.call-start = ((), (), s32[]{:S(2)}) async-start(), calls=%async_computation.1 | async-start | bytes 7077888 | tf_op jit(solution)/shard_map/all_gather | solution.py:133
  116.2 153.6 %copy-start.4 = (s32[1536]{0:T(1024)S(1)}, s32[1536]{0:T(1024)}, u32[]{:S(2)}) copy-start(s32[1536]{0:T(1024)} %param.22) | copy-start | bytes 18436
Sparse Core Ops, SparseCore 0:
  67.9 43.7 all-reduce.2
  116.2 99.0 all-gather.1

commit v2 on v1

v2 whole, which is shorter than its diff:
```python
import functools
import math

import jax
import jax.numpy as jnp
from jax import lax
from jax.experimental import pallas as pl
from jax.experimental.pallas import tpu as pltpu
from jax.sharding import PartitionSpec as P

HEAD_DIM = 64


ROPE_THETA = 10000000.0
NORM_EPS = 1e-05
NEG_FILL = -1e30
ATTN_SCALE = 0.015625
RESID_SCALE = 5.0
LOGIT_SCALE = 0.125


def rms_norm(values, gain_vec):
    return (
        values * lax.rsqrt(jnp.mean(values * values, axis=-1, keepdims=True) + NORM_EPS) * gain_vec
    )


def rotate(values, positions):
    half_dim = values.shape[-1] // 2
    inverse = jnp.exp(
        jnp.arange(half_dim, dtype=jnp.float32) * (-2.0 * math.log(ROPE_THETA) / values.shape[-1])
    )
    angles = positions.astype(jnp.float32)[:, None] * inverse[None, :]
    cos_val = jnp.cos(angles)[:, None, :]
    sine_val = jnp.sin(angles)[:, None, :]
    lower_half = values[..., :half_dim]
    upper_half = values[..., half_dim:]
    return jnp.concatenate(
        [
            lower_half * cos_val - upper_half * sine_val,
            upper_half * cos_val + lower_half * sine_val,
        ],
        axis=-1,
    )


def enter(peers):
    barrier = pltpu.get_barrier_semaphore()
    for peer in peers:
        pl.semaphore_signal(barrier, inc=1, device_id=peer, device_id_type=pl.DeviceIdType.MESH)
    pl.semaphore_wait(barrier, len(peers))


def remote(src, dst, send_sem, recv_sem, peer):
    return pltpu.make_async_remote_copy(
        src_ref=src,
        dst_ref=dst,
        send_sem=send_sem,
        recv_sem=recv_sem,
        device_id=peer,
        device_id_type=pl.DeviceIdType.MESH,
    )


def seq_peer(kv_index, seq_index, step, seq_size):
    return {"kv": kv_index, "seq": lax.rem(seq_index + step, seq_size)}


def kv_peer(kv_index, seq_index, step, kv_size):
    return {"kv": lax.rem(kv_index + step, kv_size), "seq": seq_index}


def key_kernel(seq_size, reach, packed_ref, out_ref, local_sem, send_sem, recv_sem):
    kv_index, seq_index = lax.axis_index("kv"), lax.axis_index("seq")
    own = pltpu.make_async_copy(packed_ref, out_ref.at[reach], local_sem)
    own.start()
    enter([seq_peer(kv_index, seq_index, seq_size - d, seq_size) for d in range(1, reach + 1)])
    copies = []
    for d in range(1, reach + 1):
        copies.append(
            remote(
                packed_ref,
                out_ref.at[reach - d],
                send_sem.at[d - 1],
                recv_sem.at[d - 1],
                seq_peer(kv_index, seq_index, d, seq_size),
            )
        )
    for copy in copies:
        copy.start()
    own.wait()
    for copy in copies:
        copy.wait()


def gather_keys(packed, seq_size, reach):
    return pl.pallas_call(
        lambda *refs: key_kernel(seq_size, reach, *refs),
        out_shape=jax.ShapeDtypeStruct((reach + 1,) + packed.shape, packed.dtype),
        in_specs=[pl.BlockSpec(memory_space=pltpu.VMEM)],
        out_specs=pl.BlockSpec(memory_space=pltpu.VMEM),
        scratch_shapes=[
            pltpu.SemaphoreType.DMA,
            pltpu.SemaphoreType.DMA((reach,)),
            pltpu.SemaphoreType.DMA((reach,)),
        ],
        compiler_params=pltpu.CompilerParams(
            collective_id=0, has_side_effects=True, vmem_limit_bytes=40 * 2**20
        ),
    )(packed)


def block_plan(sizes, order):
    blocks = [(dict.fromkeys(order, 0), -1)]
    for level, dim in enumerate(order):
        fresh = []
        for place, _ in blocks:
            for step in range(1, sizes[dim]):
                fresh.append(({**place, dim: step}, level))
        blocks = blocks + fresh
    return blocks


def row_kernel(
    kv_size, seq_size, part_ref, hidden_ref, gain_ref, out_ref, heard, rs_send, rs_recv, send_sem, recv_sem
):
    kv_index, seq_index = lax.axis_index("kv"), lax.axis_index("seq")
    width = out_ref.shape[2]
    half = width // 2
    cores = 2 if kv_size % 2 == 0 else 1
    x_size = kv_size // cores
    y_size = x_size if seq_size % x_size == 0 else 1
    sizes = {"z": seq_size // y_size, "y": y_size, "x": x_size, "c": cores}
    mine = {
        "z": seq_index // y_size,
        "y": lax.rem(seq_index, y_size),
        "x": kv_index // cores,
        "c": lax.rem(kv_index, cores),
    }

    def at(place):
        now = {d: lax.rem(mine[d] + place[d], sizes[d]) if place[d] else mine[d] for d in sizes}
        return now["x"] * cores + now["c"], now["z"] * y_size + now["y"]

    def moved(dim, step):
        kv_at, seq_at = at({**dict.fromkeys(sizes, 0), dim: step})
        return {"kv": kv_at, "seq": seq_at}

    def slot(place):
        kv_at, seq_at = at(place)
        return seq_at * kv_size + kv_at

    peers = [kv_peer(kv_index, seq_index, step, kv_size) for step in range(1, kv_size)]
    peers += [moved(d, step) for d in ("z", "y") for step in range(1, sizes[d])]
    enter(peers)
    shares = []
    for step in range(1, kv_size):
        peer = kv_peer(kv_index, seq_index, step, kv_size)
        shares.append(
            remote(
                part_ref.at[peer["kv"]],
                heard.at[step - 1],
                rs_send.at[step - 1],
                rs_recv.at[step - 1],
                peer,
            )
        )
    for share in shares:
        share.start()
    total = part_ref[kv_index].astype(jnp.float32)
    for step, share in enumerate(shares):
        share.wait_recv()
        total = total + heard[step].astype(jnp.float32)
    values = hidden_ref[...].astype(jnp.float32) + RESID_SCALE * total
    out_ref[seq_index * kv_size + kv_index] = rms_norm(values, gain_ref[...]).astype(out_ref.dtype)

    orders = (("z", "y", "x", "c"), ("z", "x", "y", "c"))
    plans = [block_plan(sizes, order) for order in orders]
    sent = []
    used = [0, 0]
    for turn in range(kv_size * seq_size):
        for part in range(2):
            place, level = plans[part][turn]
            index = slot(place)
            view = out_ref.at[index, :, pl.ds(part * half, half)]
            if level >= 0:
                remote(
                    view, view, send_sem.at[part, 0], recv_sem.at[part, index], peers[0]
                ).wait_recv()
            for dim in orders[part][level + 1 :]:
                for step in range(1, sizes[dim]):
                    copy = remote(
                        view,
                        view,
                        send_sem.at[part, used[part]],
                        recv_sem.at[part, index],
                        moved(dim, step),
                    )
                    copy.start()
                    used[part] += 1
                    sent.append(copy)
    for copy in sent:
        copy.wait_send()
    for share in shares:
        share.wait_send()


def gather_rows(part, hidden, gain, kv_size, seq_size):
    _, rows, width = part.shape
    count = kv_size * seq_size
    return pl.pallas_call(
        lambda *refs: row_kernel(kv_size, seq_size, *refs),
        out_shape=jax.ShapeDtypeStruct((count, rows, width), jnp.bfloat16),
        in_specs=[pl.BlockSpec(memory_space=pltpu.VMEM)] * 3,
        out_specs=pl.BlockSpec(memory_space=pltpu.VMEM),
        scratch_shapes=[
            pltpu.VMEM((kv_size - 1, rows, width), jnp.bfloat16),
            pltpu.SemaphoreType.DMA((kv_size - 1,)),
            pltpu.SemaphoreType.DMA((kv_size - 1,)),
            pltpu.SemaphoreType.DMA((2, count)),
            pltpu.SemaphoreType.DMA((2, count)),
        ],
        compiler_params=pltpu.CompilerParams(
            collective_id=1, has_side_effects=True, vmem_limit_bytes=48 * 2**20
        ),
    )(part, hidden, gain)


def merge(stats):
    top = stats[0][0:1]
    for item in stats[1:]:
        top = jnp.maximum(top, item[0:1])
    total = spread = target = jnp.zeros_like(top)
    for item in stats:
        rescale = jnp.exp(item[0:1] - top)
        total = total + rescale * item[1:2]
        spread = spread + rescale * (item[2:3] + (item[0:1] - top) * item[1:2])
        target = target + item[3:4]
    return jnp.concatenate([top, total, spread, target], axis=0)


def stat_kernel(
    kv_size, seq_size, stat_ref, out_ref, near, block, far, send_one, recv_one, send_two, recv_two
):
    kv_index, seq_index = lax.axis_index("kv"), lax.axis_index("seq")
    by_seq = [seq_peer(kv_index, seq_index, step, seq_size) for step in range(1, seq_size)]
    by_kv = [kv_peer(kv_index, seq_index, step, kv_size) for step in range(1, kv_size)]
    enter(by_seq + by_kv)
    first = [
        remote(stat_ref.at[peer["seq"]], near.at[i], send_one.at[i], recv_one.at[i], peer)
        for i, peer in enumerate(by_seq)
    ]
    for copy in first:
        copy.start()
    for copy in first:
        copy.wait()
    block[...] = merge([stat_ref[seq_index]] + [near[i] for i in range(seq_size - 1)])
    second = [
        remote(block, far.at[i], send_two.at[i], recv_two.at[i], peer)
        for i, peer in enumerate(by_kv)
    ]
    for copy in second:
        copy.start()
    for copy in second:
        copy.wait()
    out_ref[...] = merge([block[...]] + [far[i] for i in range(kv_size - 1)])


def merge_stats(stats, kv_size, seq_size):
    one = stats.shape[1:]
    return pl.pallas_call(
        lambda *refs: stat_kernel(kv_size, seq_size, *refs),
        out_shape=jax.ShapeDtypeStruct(one, jnp.float32),
        in_specs=[pl.BlockSpec(memory_space=pltpu.VMEM)],
        out_specs=pl.BlockSpec(memory_space=pltpu.VMEM),
        scratch_shapes=[
            pltpu.VMEM((seq_size - 1,) + one, jnp.float32),
            pltpu.VMEM(one, jnp.float32),
            pltpu.VMEM((kv_size - 1,) + one, jnp.float32),
            pltpu.SemaphoreType.DMA((seq_size - 1,)),
            pltpu.SemaphoreType.DMA((seq_size - 1,)),
            pltpu.SemaphoreType.DMA((kv_size - 1,)),
            pltpu.SemaphoreType.DMA((kv_size - 1,)),
        ],
        compiler_params=pltpu.CompilerParams(
            collective_id=2, has_side_effects=True, vmem_limit_bytes=32 * 2**20
        ),
    )(stats)


def local(
    kv_size,
    seq_size,
    hidden_states,
    attn_gain,
    w_q,
    w_k,
    w_v,
    w_o,
    final_gain,
    w_head,
    doc_lengths,
    target_ids,
    vocab_mask,
):
    tok_rows = hidden_states.shape[0]
    seq_index = lax.axis_index("seq")
    kv_local = w_k.shape[1] // HEAD_DIM
    q_local = w_q.shape[1] // HEAD_DIM
    group_size = q_local // kv_local
    key_width = kv_local * HEAD_DIM
    stream = hidden_states.astype(jnp.float32)
    normed_in = rms_norm(stream, attn_gain).astype(jnp.bfloat16)
    queries = jnp.dot(normed_in, w_q, preferred_element_type=jnp.float32)
    key_proj = jnp.dot(normed_in, w_k, preferred_element_type=jnp.float32)
    value_proj = jnp.dot(normed_in, w_v, preferred_element_type=jnp.float32)
    token_pos = seq_index * tok_rows + jnp.arange(tok_rows, dtype=jnp.int32)
    docs = jnp.arange(doc_lengths.shape[0], dtype=jnp.int32)
    doc_starts = jnp.sum(jnp.where(docs[None, :] < docs[:, None], doc_lengths[None, :], 0), axis=1)
    doc_start = jnp.max(
        jnp.where(doc_starts[None, :] <= token_pos[:, None], doc_starts[None, :], 0), axis=1
    )
    positions = token_pos - doc_start
    rotated_q = rotate(queries.reshape(tok_rows, q_local, HEAD_DIM), positions).astype(jnp.bfloat16)
    rotated_q = rotated_q.reshape(tok_rows, kv_local, group_size, HEAD_DIM)
    rotated_k = rotate(key_proj.reshape(tok_rows, kv_local, HEAD_DIM), positions).astype(
        jnp.bfloat16
    )
    packed = jnp.concatenate(
        [rotated_k.reshape(tok_rows, key_width), value_proj.astype(jnp.bfloat16)], axis=1
    )
    reach = (seq_size + 1) // 2
    key_blocks = gather_keys(packed, seq_size, reach)
    row_count = (reach + 1) * tok_rows
    shard_rows = key_blocks.reshape(row_count, 2 * key_width)
    key_pos = (seq_index - reach) * tok_rows + jnp.arange(row_count, dtype=jnp.int32)
    key_rows = shard_rows[:, :key_width].reshape(row_count, kv_local, HEAD_DIM)
    value_rows = shard_rows[:, key_width:].reshape(row_count, kv_local, HEAD_DIM)
    scores = (
        jnp.einsum("tkgd,skd->kgts", rotated_q, key_rows, preferred_element_type=jnp.float32)
        * ATTN_SCALE
    )
    allowed = (key_pos[None, :] >= doc_start[:, None]) & (key_pos[None, :] <= token_pos[:, None])
    scores = jnp.where(allowed, scores, NEG_FILL)
    top_score = jnp.max(scores, axis=-1)
    weights = jnp.where(allowed, jnp.exp(scores - top_score[..., None]), 0.0)
    totals = jnp.sum(weights, axis=-1)
    context_sum = jnp.einsum(
        "kgts,skd->kgtd",
        weights.astype(jnp.bfloat16),
        value_rows,
        preferred_element_type=jnp.float32,
    )
    context = (
        (context_sum / totals[..., None])
        .transpose(2, 0, 1, 3)
        .reshape(tok_rows, q_local * HEAD_DIM)
        .astype(jnp.bfloat16)
    )
    vocab_local = w_head.shape[1]
    flat_rank = lax.axis_index(("kv", "seq"))
    live_mask = vocab_mask == 1
    columns = flat_rank * vocab_local + jnp.arange(vocab_local, dtype=jnp.int32)
    own_rows = tok_rows // kv_size
    part = jnp.dot(context, w_o, preferred_element_type=jnp.float32).astype(jnp.bfloat16)
    own_hidden = lax.dynamic_slice_in_dim(
        hidden_states, lax.axis_index("kv") * own_rows, own_rows, 0
    )
    head_shard_rows = gather_rows(
        part.reshape(kv_size, own_rows, part.shape[1]),
        own_hidden,
        final_gain[None, :],
        kv_size,
        seq_size,
    ).reshape(tok_rows * seq_size, part.shape[1])
    logits = jnp.dot(head_shard_rows, w_head, preferred_element_type=jnp.float32) * LOGIT_SCALE
    masked = jnp.where(live_mask[None, :], logits, NEG_FILL)
    top_row = jnp.max(masked, axis=1)
    shifted = jnp.where(live_mask[None, :], masked - top_row[:, None], 0.0)
    expw = jnp.where(live_mask[None, :], jnp.exp(shifted), 0.0)
    target = jnp.sum(jnp.where(target_ids[:, None] == columns[None, :], logits, 0.0), axis=1)
    row_stats = jnp.stack([top_row, jnp.sum(expw, axis=1), jnp.sum(expw * shifted, axis=1), target])
    blocks = row_stats.reshape(4, seq_size, tok_rows).transpose(1, 0, 2)
    top_all, total_all, spread_all, target_all = merge_stats(blocks, kv_size, seq_size)
    log_probs = target_all - top_all - jnp.log(total_all)
    entropies = jnp.log(total_all) - spread_all / total_all
    return (log_probs, entropies)


def solution(mesh):
    in_specs = (
        P("seq", None),
        P(),
        P(None, "kv"),
        P(None, "kv"),
        P(None, "kv"),
        P("kv", None),
        P(),
        P(None, ("kv", "seq")),
        P(),
        P(),
        P(("kv", "seq")),
    )
    out_specs = (P("seq"), P("seq"))
    sizes = (mesh.shape["kv"], mesh.shape["seq"])
    return jax.shard_map(functools.partial(local, *sizes), mesh=mesh, in_specs=in_specs, out_specs=out_specs, check_vma=False)
```

time: 326 us -> 127 us (0.39)
  waiting for transfers between devices: 143 us -> 0 us
  blocking collectives: 116 us -> 0 us
  Pallas kernels: 0 us -> 81.9 us
  between operations: 15.6 us -> 0.88 us
  other arithmetic: 17.9 us -> 10.4 us
    all_gather x1 -> x0, waiting for transfers between devices: 99.2 us -> none  [local(): head_shard_rows = lax.all_gather(final_in, 'seq', axis=0, tiled=True)]
    pallas_call x0 -> x3, Pallas kernels: none -> 81.9 us  [the longest x1 49.7 us: gather_rows(): pl.pallas_call(lambda *refs: row_kernel(kv_size, seq_size, *refs), out_sh...]
    psum x1 -> x0, waiting for transfers between devices: 43.7 us -> none  [local(): lax.psum(jnp.dot(context, w_o, preferred_element_type=jnp.float32), 'kv')]
    psum x1 -> x0, blocking collectives: 41.1 us -> none  [local(): lax.psum((row_stats[1] * rescale, rescale * (row_stats[2] + (row_stats[0]...]
    pmax x1 -> x0, blocking collectives: 38.4 us -> none  [local(): top_all = lax.pmax(row_stats[0], ('kv', 'seq'))]
    all_gather x1 -> x0, blocking collectives: 36 us -> none  [local(): shard_rows = lax.all_gather(packed, 'seq', axis=0, tiled=True)]
    sub x0 -> x1, matrix products: none -> 5.34 us  [local(): weights = jnp.where(allowed, jnp.exp(scores - top_score[..., None]), 0.0)]
    reduce_sum x2 -> x1, other arithmetic: 9.75 us -> 6.83 us  [local(): jnp.sum(expw, axis=1)]
  transfers between devices with their start and end apart: 2 -> 0, of which waited for: 2 -> 0; matrix products, arithmetic and copies ran while one was open for 0% -> 0% of each run, Pallas kernels for 0% -> 0%
where the time goes in v2:
time: 127 us
  Pallas kernels  81.9 us (64%)
  matrix products  31 us (24%)
  other arithmetic  10.4 us (8%)
  local copies, waits for them, and re-layouts  2.46 us (2%)
    pallas_call x1, Pallas kernels, gather_rows(): pl.pallas_call(lambda *refs: row_kernel(kv_size, seq_size, *refs), out_sh...  49.7 us
    pallas_call x1, Pallas kernels, gather_keys(): pl.pallas_call(lambda *refs: key_kernel(seq_size, reach, *refs), out_shap...  17.6 us
    dot_general x1, matrix products, local(): jnp.dot(head_shard_rows, w_head, preferred_element_type=jnp.float32)  16 us
    pallas_call x1, Pallas kernels, merge_stats(): pl.pallas_call(lambda *refs: stat_kernel(kv_size, seq_size, *refs), out_s...  14.5 us
    reduce_sum x1, other arithmetic, local(): jnp.sum(expw, axis=1)  6.83 us
    sub x1, matrix products, local(): weights = jnp.where(allowed, jnp.exp(scores - top_score[..., None]), 0.0)  5.34 us
    dot_general x1, matrix products, local(): jnp.einsum('kgts,skd->kgtd', weights.astype(jnp.bfloat16), value_rows, pr...  3.01 us
    dot_general x1, matrix products, local(): queries = jnp.dot(normed_in, w_q, preferred_element_type=jnp.float32)  2.58 us

profile of v2, /device:TPU:0, one launch (start us, length us, event | category | flops | bytes accessed | tf_op | source)
XLA Modules:
  0.0 126.7 jit_solution(8330976120738829249)
XLA Ops:
  0.7 0.9 select_reduce_fusion.3
  1.6 0.1 select_reduce_fusion.2
  1.7 0.2 multiply_cosine_fusion
  1.9 1.4 %fusion.8 = f32[192]{0:T(256)S(1)} fusion(bf16[192,2048]{1,0:T(8,128)(2,1)} %param.11), kind=kLoop, calls=%fused_computation.19 | loop fusion | flops 1179456 | bytes 787200 | tf_op jit(solution)/shard_map/reduce_sum | solution.py:24
  3.3 1.8 %fusion.32 = f32[192,128]{0,1:T(8,128)S(1)} fusion(bf16[2048,128]{1,0:T(8,128)(2,1)} %param.14, bf16[192,2048]{1,0:T(8,128)(2,1)} %param.11, f32[2048]{0:T(1024)} %param.12, f32[192]{0:T(256)S(1)} %add_rsqrt_fusion), kind=kOutput, calls=%fused_computation.57 | convolution fusion | flops 102236160 | bytes 1417984 | tf_op jit(solution)/shard_map/dot_general | solution.py:315
  5.2 0.1 copy.23
  5.3 1.7 %convolution_convert_fusion.1 = bf16[192,128]{1,0:T(8,128)(2,1)S(1)} fusion(bf16[2048,128]{1,0:T(8,128)(2,1)} %param.15, bf16[192,2048]{1,0:T(8,128)(2,1)} %param.11, f32[2048]{0:T(1024)} %param.12, f32[192]{0:T(256)S(1)} %add_rsqrt_fusion), kind=kOutput, calls=%fused_computation.25 | convolution fusion | flops 102260736 | bytes 1368832 | tf_op jit(solution)/shard_map/dot_general | solution.py:316
  7.0 17.6 %shard_map.122 = bf16[5,192,256]{2,1,0:T(8,128)(2,1)S(1)} custom-call(bf16[192,256]{1,0:T(8,128)(2,1)S(1)} %pad_maximum_fusion.7.refs_0_), custom_call_target="tpu_custom_call" | custom-call | tf_op jit(solution)/shard_map/pallas_call | solution.py:97
  24.7 0.9 copy.24
  25.6 2.6 %fusion.29 = f32[192,512]{0,1:T(8,128)S(1)} fusion(bf16[2048,512]{1,0:T(8,128)(2,1)} %param.13, bf16[192,2048]{1,0:T(8,128)(2,1)S(1)} %copy-done.2, f32[2048]{0:T(1024)S(1)} %copy-done.5, f32[192]{0:T(256)S(1)} %add_rsqrt_fusion), kind=kOutput, calls=%fused_computation.56 | convolution fusion | flops 404226048 | bytes 3285760 | tf_op jit(solution)/shard_map/dot_general | solution.py:314
  28.3 0.2 compare_and_fusion
  28.5 5.3 %fusion.35 = (f32[2,4,192]{2,1,0:T(4,128)S(1)}, bf16[2,4,192,960]{3,2,1,0:T(8,128)(2,1)}) fusion(pred[192,960]{1,0:T(8,128)(4,1)S(1)} %compare_and_fusion, bf16[960,2,64,1]{0,2,3,1:T(8,128)(2,1)} %bitcast.60, bf16[192,2,4,32]{0,3,2,1:T(8,128)(2,1)S(1)} %bitcast.64, bf16[192,2,4,32]{0,3,2,1:T(8,128)(2,1)S(1)} %bitcast.63), kind=kOutput, calls=%fused_computation.59 | convolution fusion | flops 197985216 | bytes 3581952 | tf_op jit(solution)/shard_map/sub | solution.py:346
  33.9 0.1 copy.26
  34.0 3.0 %fusion.17 = bf16[192,2,4,64]{0,3,2,1:T(8,128)(2,1)S(1)} fusion(bf16[960,2,64,1]{0,2,3,1:T(8,128)(2,1)S(1)} %bitcast.61, bf16[2,4,192,960]{3,2,1,0:T(8,128)(2,1)} %get-tuple-element.16, f32[192,2,4]{0,2,1:T(4,128)S(1)} %bitcast.67), kind=kOutput, calls=%fused_computation.24 | convolution fusion | flops 188940288 | bytes 3397632 | tf_op jit(solution)/shard_map/kgts,skd->kgtd/dot_general | solution.py:348
  37.0 0.6 convolution_convert_fusion
  37.7 0.9 constant_dynamic-slice_fusion.refs_1_
  38.6 49.7 %shard_map.123 = bf16[32,48,2048]{2,1,0:T(8,128)(2,1)} custom-call(bf16[4,48,2048]{2,1,0:T(8,128)(2,1)S(1)} %bitcast.53, bf16[48,2048]{1,0:T(8,128)(2,1)S(1)} %constant_dynamic-slice_fusion.refs_1_, f32[1,2048]{1,0:T(1,128)S(1)} %bitcast.55), custom_call_target="tpu_custom_call" | custom-call | tf_op jit(solution)/shard_map/pallas_call | solution.py:211
  88.4 16.0 %select_reduce_fusion.1 = (f32[1536]{0:T(1024)S(1)}, f32[1536,1544]{0,1:T(8,128)}) fusion(pred[1544]{0:T(1024)(128)(4,1)S(1)} %broadcast_compare_fusion, bf16[1536,2048]{1,0:T(8,128)(2,1)} %bitcast.56, bf16[2048,1544]{0,1:T(8,128)(2,1)} %param.18), kind=kOutput, calls=%fused_computation.7 | convolution fusion | flops 9721120768 | bytes 22109704 | tf_op jit(solution)/shard_map/dot_general | solution.py:376
  104.4 6.8 %fusion.1 = (f32[1536]{0:T(1024)S(1)}, f32[1536]{0:T(1024)S(1)}, f32[1536]{0:T(1024)S(1)}) fusion(f32[1536,1544]{0,1:T(8,128)} %get-tuple-element.18, f32[1536]{0:T(1024)S(1)} %get-tuple-element.17, pred[1544]{0:T(1024)(128)(4,1)S(1)} %broadcast_compare_fusion, s32[1544]{0:T(1024)S(1)} %iota_add_fusion, s32[1536]{0:T(1024)S(1)} %copy-done.4), kind=kLoop, calls=%fused_computation.5 | loop fusion | flops 23711232 | bytes 9524776 | tf_op jit(solution)/shard_map/reduce_sum | solution.py:382
  111.2 0.1 stack.16
  111.3 0.1 stack.17
  111.4 0.1 stack.18
  111.6 14.5 %shard_map.124 = f32[4,192]{1,0:T(4,128)S(1)} custom-call(f32[8,4,192]{2,1,0:T(4,128)S(1)} %maximum_bitcast_fusion.refs_0_), custom_call_target="tpu_custom_call" | custom-call | tf_op jit(solution)/shard_map/pallas_call | solution.py:271
  126.1 0.6 divide_subtract_fusion
  (26 shorter events, 0.4 us)
Async XLA Ops:
  0.6 36.4 %copy-start = (bf16[512,2048]{1,0:T(8,128)(2,1)S(1)}, bf16[512,2048]{1,0:T(8,128)(2,1)}, u32[]{:S(2)}) copy-start(bf16[512,2048]{1,0:T(8,128)(2,1)} %param.16) | copy-start | bytes 6291460
  0.6 25.0 %copy-start.2 = (bf16[192,2048]{1,0:T(8,128)(2,1)S(1)}, bf16[192,2048]{1,0:T(8,128)(2,1)}, u32[]{:S(2)}) copy-start(bf16[192,2048]{1,0:T(8,128)(2,1)} %param.11) | copy-start | bytes 2359300
  0.7 24.9 %copy-start.5 = (f32[2048]{0:T(1024)S(1)}, f32[2048]{0:T(1024)}, u32[]{:S(2)}) copy-start(f32[2048]{0:T(1024)} %param.12) | copy-start | bytes 24580
  33.9 4.8 %copy-start.1 = (f32[2048]{0:T(1024)S(1)}, f32[2048]{0:T(1024)}, u32[]{:S(2)}) copy-start(f32[2048]{0:T(1024)} %param.17) | copy-start | bytes 24580
  37.0 51.3 %copy-start.3 = (s32[1544]{0:T(1024)S(1)}, s32[1544]{0:T(1024)}, u32[]{:S(2)}) copy-start(s32[1544]{0:T(1024)} %param.21) | copy-start | bytes 18532
  88.4 16.0 %copy-start.4 = (s32[1536]{0:T(1024)S(1)}, s32[1536]{0:T(1024)}, u32[]{:S(2)}) copy-start(s32[1536]{0:T(1024)} %param.20) | copy-start | bytes 18436

commit v3 on v2

--- a/solution.py
+++ b/solution.py
@@ -203,6 +203,199 @@
         copy.wait_send()
     for share in shares:
         share.wait_send()
+
+
+def head_kernel(
+    kv_size,
+    seq_size,
+    part_ref,
+    hidden_ref,
+    gain_ref,
+    target_ref,
+    live_ref,
+    column_ref,
+    head_ref,
+    stat_ref,
+    held,
+    head,
+    scored,
+    heard,
+    head_sem,
+    rs_send,
+    rs_recv,
+    send_sem,
+    recv_sem,
+):
+    kv_index, seq_index = lax.axis_index("kv"), lax.axis_index("seq")
+    width = held.shape[2]
+    half = width // 2
+    rows = held.shape[1]
+    weights = pltpu.make_async_copy(head_ref, head, head_sem)
+    weights.start()
+    cores = 2 if kv_size % 2 == 0 else 1
+    x_size = kv_size // cores
+    y_size = x_size if seq_size % x_size == 0 else 1
+    sizes = {"z": seq_size // y_size, "y": y_size, "x": x_size, "c": cores}
+    mine = {
+        "z": seq_index // y_size,
+        "y": lax.rem(seq_index, y_size),
+        "x": kv_index // cores,
+        "c": lax.rem(kv_index, cores),
+    }
+
+    def at(place):
+        now = {d: lax.rem(mine[d] + place[d], sizes[d]) if place[d] else mine[d] for d in sizes}
+        return now["x"] * cores + now["c"], now["z"] * y_size + now["y"]
+
+    def moved(dim, step):
+        kv_at, seq_at = at({**dict.fromkeys(sizes, 0), dim: step})
+        return {"kv": kv_at, "seq": seq_at}
+
+    def slot(place):
+        kv_at, seq_at = at(place)
+        column = (kv_at // cores) * y_size + lax.rem(seq_at, y_size)
+        return (column * sizes["z"] + seq_at // y_size) * cores + lax.rem(kv_at, cores)
+
+    peers = [kv_peer(kv_index, seq_index, step, kv_size) for step in range(1, kv_size)]
+    peers += [moved(d, step) for d in ("z", "y") for step in range(1, sizes[d])]
+    enter(peers)
+    shares = []
+    for step in range(1, kv_size):
+        peer = kv_peer(kv_index, seq_index, step, kv_size)
+        shares.append(
+            remote(
+                part_ref.at[peer["kv"]],
+                heard.at[step - 1],
+                rs_send.at[step - 1],
+                rs_recv.at[step - 1],
+                peer,
+            )
+        )
+    for share in shares:
+        share.start()
+    total = part_ref[kv_index].astype(jnp.float32)
+    for step, share in enumerate(shares):
+        share.wait_recv()
+        total = total + heard[step].astype(jnp.float32)
+    values = hidden_ref[...].astype(jnp.float32) + RESID_SCALE * total
+    held[slot(dict.fromkeys(sizes, 0))] = rms_norm(values, gain_ref[...]).astype(held.dtype)
+
+    orders = (("z", "y", "x", "c"), ("z", "x", "y", "c"))
+    sent = []
+    used = [0, 0]
+
+    def arrive(part, place):
+        index = slot(place)
+        view = held.at[index, :, pl.ds(part * half, half)]
+        level = max([n for n, dim in enumerate(orders[part]) if place[dim]], default=-1)
+        if level >= 0:
+            remote(
+                view, view, send_sem.at[part, 0], recv_sem.at[part, index], peers[0]
+            ).wait_recv()
+        for dim in orders[part][level + 1 :]:
+            for step in range(1, sizes[dim]):
+                copy = remote(
+                    view,
+                    view,
+                    send_sem.at[part, used[part]],
+                    recv_sem.at[part, index],
+                    moved(dim, step),
+                )
+                copy.start()
+                used[part] += 1
+                sent.append(copy)
+
+    depth = sizes["z"] * cores
+    high = depth * rows
+    total_columns = head.shape[1]
+    cuts = [*range(0, total_columns - 511, 512)]
+    tiles = list(zip(cuts, cuts[1:] + [total_columns])) if cuts else [(0, total_columns)]
+
+    def score(x_step, y_step):
+        first = slot({"z": 0, "y": y_step, "x": x_step, "c": 0}) // depth
+        block = held[pl.ds(first * depth, depth)].reshape(high, width)
+        wanted = jnp.broadcast_to(target_ref[first], (128, high)).T[:, 0:1]
+        top = jnp.full((high, 1), NEG_FILL, jnp.float32)
+        target = jnp.zeros((high, 1), jnp.float32)
+        for low, end in tiles:
+            logits = (
+                jnp.dot(block, head[:, low:end], preferred_element_type=jnp.float32) * LOGIT_SCALE
+            )
+            masked = jnp.where(live_ref[:, low:end] == 1, logits, NEG_FILL)
+            scored[:, low:end] = masked
+            top = jnp.maximum(top, jnp.max(masked, axis=1, keepdims=True))
+            hit = column_ref[:, low:end] == wanted
+            target = target + jnp.sum(jnp.where(hit, logits, 0.0), axis=1, keepdims=True)
+        total = jnp.zeros((high, 1), jnp.float32)
+        spread = jnp.zeros((high, 1), jnp.float32)
+        for low, end in tiles:
+            shifted = scored[:, low:end] - top
+            expw = jnp.exp(shifted)
+            total = total + jnp.sum(expw, axis=1, keepdims=True)
+            spread = spread + jnp.sum(expw * shifted, axis=1, keepdims=True)
+        lane = lax.broadcasted_iota(jnp.int32, (high, 128), 1)
+        table = jnp.where(lane == 0, top, jnp.where(lane == 1, total, jnp.where(lane == 2, spread, target)))
+        stat_ref[first] = table.T[0:8]
+
+    spots = [(i, j) for i in range(x_size) for j in range(y_size)]
+    for stage in range(3):
+        now = [spot for spot in spots if (spot[0] > 0) + (spot[1] > 0) == stage]
+        for z_step in range(sizes["z"]):
+            for i, j in now:
+                for part in range(2):
+                    arrive(part, {"z": z_step, "y": j, "x": i, "c": 0})
+        if stage == 0:
+            weights.wait()
+        for i, j in now:
+            for z_step in range(sizes["z"]):
+                for c_step in range(1, cores):
+                    for part in range(2):
+                        arrive(part, {"z": z_step, "y": j, "x": i, "c": c_step})
+            score(i, j)
+    for copy in sent:
+        copy.wait_send()
+    for share in shares:
+        share.wait_send()
+
+
+def split_of(kv_size, seq_size):
+    cores = 2 if kv_size % 2 == 0 else 1
+    x_size = kv_size // cores
+    y_size = x_size if seq_size % x_size == 0 else 1
+    return seq_size // y_size, y_size, x_size, cores
+
+
+def score_rows(part, hidden, gain, target_ids, live, columns, head, kv_size, seq_size):
+    _, rows, width = part.shape
+    count = kv_size * seq_size
+    z_size, y_size, x_size, cores = split_of(kv_size, seq_size)
+    spots = x_size * y_size
+    high = z_size * cores * rows
+    targets = target_ids.reshape(z_size, y_size, x_size, cores * rows)
+    targets = targets.transpose(2, 1, 0, 3).reshape(spots, 1, high)
+    stats = pl.pallas_call(
+        lambda *refs: head_kernel(kv_size, seq_size, *refs),
+        out_shape=jax.ShapeDtypeStruct((spots, 8, high), jnp.float32),
+        in_specs=[pl.BlockSpec(memory_space=pltpu.VMEM)] * 6
+        + [pl.BlockSpec(memory_space=pl.ANY)],
+        out_specs=pl.BlockSpec(memory_space=pltpu.VMEM),
+        scratch_shapes=[
+            pltpu.VMEM((count, rows, width), jnp.bfloat16),
+            pltpu.VMEM(head.shape, jnp.bfloat16),
+            pltpu.VMEM((high, head.shape[1]), jnp.float32),
+            pltpu.VMEM((kv_size - 1, rows, width), jnp.bfloat16),
+            pltpu.SemaphoreType.DMA,
+            pltpu.SemaphoreType.DMA((kv_size - 1,)),
+            pltpu.SemaphoreType.DMA((kv_size - 1,)),
+            pltpu.SemaphoreType.DMA((2, count)),
+            pltpu.SemaphoreType.DMA((2, count)),
+        ],
+        compiler_params=pltpu.CompilerParams(
+            collective_id=3, has_side_effects=True, vmem_limit_bytes=48 * 2**20
+        ),
+    )(part, hidden, gain, targets, live, columns, head)
+    stats = stats[:, :4].reshape(x_size, y_size, 4, z_size, cores * rows)
+    return stats.transpose(3, 1, 2, 0, 4).reshape(seq_size, 4, kv_size * rows)
 
 
 def gather_rows(part, hidden, gain, kv_size, seq_size):
@@ -366,21 +559,34 @@
     own_hidden = lax.dynamic_slice_in_dim(
         hidden_states, lax.axis_index("kv") * own_rows, own_rows, 0
     )
-    head_shard_rows = gather_rows(
-        part.reshape(kv_size, own_rows, part.shape[1]),
-        own_hidden,
-        final_gain[None, :],
-        kv_size,
-        seq_size,
-    ).reshape(tok_rows * seq_size, part.shape[1])
-    logits = jnp.dot(head_shard_rows, w_head, preferred_element_type=jnp.float32) * LOGIT_SCALE
-    masked = jnp.where(live_mask[None, :], logits, NEG_FILL)
-    top_row = jnp.max(masked, axis=1)
-    shifted = jnp.where(live_mask[None, :], masked - top_row[:, None], 0.0)
-    expw = jnp.where(live_mask[None, :], jnp.exp(shifted), 0.0)
-    target = jnp.sum(jnp.where(target_ids[:, None] == columns[None, :], logits, 0.0), axis=1)
-    row_stats = jnp.stack([top_row, jnp.sum(expw, axis=1), jnp.sum(expw * shifted, axis=1), target])
-    blocks = row_stats.reshape(4, seq_size, tok_rows).transpose(1, 0, 2)
+    if own_rows % 16 == 0:
+        blocks = score_rows(
+            part.reshape(kv_size, own_rows, part.shape[1]),
+            own_hidden,
+            final_gain[None, :],
+            target_ids,
+            vocab_mask[None, :],
+            columns[None, :],
+            w_head,
+            kv_size,
+            seq_size,
+        )
+    else:
+        head_shard_rows = gather_rows(
+            part.reshape(kv_size, own_rows, part.shape[1]),
+            own_hidden,
+            final_gain[None, :],
+            kv_size,
+            seq_size,
+        ).reshape(tok_rows * seq_size, part.shape[1])
+        logits = jnp.dot(head_shard_rows, w_head, preferred_element_type=jnp.float32) * LOGIT_SCALE
+        masked = jnp.where(live_mask[None, :], logits, NEG_FILL)
+        top_row = jnp.max(masked, axis=1)
+        shifted = jnp.where(live_mask[None, :], masked - top_row[:, None], 0.0)
+        expw = jnp.where(live_mask[None, :], jnp.exp(shifted), 0.0)
+        target = jnp.sum(jnp.where(target_ids[:, None] == columns[None, :], logits, 0.0), axis=1)
+        row_stats = jnp.stack([top_row, jnp.sum(expw, axis=1), jnp.sum(expw * shifted, axis=1), target])
+        blocks = row_stats.reshape(4, seq_size, tok_rows).transpose(1, 0, 2)
     top_all, total_all, spread_all, target_all = merge_stats(blocks, kv_size, seq_size)
     log_probs = target_all - top_all - jnp.log(total_all)
     entropies = jnp.log(total_all) - spread_all / total_all

time: 127 us -> 120 us (0.945)
  matrix products: 31 us -> 15 us
  local copies, waits for them, and re-layouts: 2.46 us -> 14.9 us
  other arithmetic: 10.4 us -> 4.25 us
  Pallas kernels: 81.9 us -> 84.8 us
    dot_general x1 -> x0, matrix products: 16 us -> none  [local(): jnp.dot(head_shard_rows, w_head, preferred_element_type=jnp.float32)]
    unnamed x12 -> x13, local copies, waits for them, and re-layouts: 0.04 us -> 9.64 us
    reduce_sum x1 -> x0, other arithmetic: 6.83 us -> none  [local(): jnp.sum(expw, axis=1)]
    pallas_call x1, Pallas kernels: 49.7 us -> 52.7 us  [score_rows(): pl.pallas_call(lambda *refs: head_kernel(kv_size, seq_size, *refs), out_s...]
    slice x2, local copies, waits for them, and re-layouts: 0.9 us -> 2.51 us  [local(): key_rows = shard_rows[:, :key_width].reshape(row_count, kv_local, HEAD_DIM)]
where the time goes in v3:
time: 120 us
  Pallas kernels  84.8 us (71%)
  matrix products  15 us (12%)
  local copies, waits for them, and re-layouts  14.9 us (12%)
  other arithmetic  4.25 us (4%)
    pallas_call x1, Pallas kernels, score_rows(): pl.pallas_call(lambda *refs: head_kernel(kv_size, seq_size, *refs), out_s...  52.7 us
    pallas_call x1, Pallas kernels, gather_keys(): pl.pallas_call(lambda *refs: key_kernel(seq_size, reach, *refs), out_shap...  17.6 us
    pallas_call x1, Pallas kernels, merge_stats(): pl.pallas_call(lambda *refs: stat_kernel(kv_size, seq_size, *refs), out_s...  14.5 us
    unnamed x13, local copies, waits for them, and re-layouts  9.64 us
    sub x1, matrix products, local(): weights = jnp.where(allowed, jnp.exp(scores - top_score[..., None]), 0.0)  5.45 us
    dot_general x1, matrix products, local(): jnp.einsum('kgts,skd->kgtd', weights.astype(jnp.bfloat16), value_rows, pr...  3.01 us
    dot_general x1, matrix products, local(): queries = jnp.dot(normed_in, w_q, preferred_element_type=jnp.float32)  2.62 us
    slice x2, local copies, waits for them, and re-layouts, local(): key_rows = shard_rows[:, :key_width].reshape(row_count, kv_local, HEAD_DIM)  2.51 us

profile of v3, /device:TPU:0, one launch (start us, length us, event | category | flops | bytes accessed | tf_op | source)
XLA Modules:
  0.0 119.8 jit_solution(1698481525132537832)
XLA Ops:
  0.7 0.9 select_reduce_fusion.1
  1.7 1.4 %fusion.7 = f32[192]{0:T(256)S(1)} fusion(bf16[192,2048]{1,0:T(8,128)(2,1)} %param.11), kind=kLoop, calls=%fused_computation.12 | loop fusion | flops 1179456 | bytes 787200 | tf_op jit(solution)/shard_map/reduce_sum | solution.py:24
  3.1 0.7 broadcast_in_dim.70.refs_4_
  3.8 0.8 reshape.142
  4.6 0.1 reshape.143.refs_3_
  4.7 1.7 %convolution_convert_fusion.1 = bf16[192,128]{1,0:T(8,128)(2,1)S(1)} fusion(bf16[2048,128]{1,0:T(8,128)(2,1)} %param.15, bf16[192,2048]{1,0:T(8,128)(2,1)} %param.11, f32[2048]{0:T(1024)} %param.12, f32[192]{0:T(256)S(1)} %add_rsqrt_fusion), kind=kOutput, calls=%fused_computation.18 | convolution fusion | flops 102260736 | bytes 1368832 | tf_op jit(solution)/shard_map/dot_general | solution.py:509
  6.4 0.2 multiply_cosine_fusion
  6.7 1.5 %fusion.31 = f32[192,128]{0,1:T(8,128)S(1)} fusion(bf16[2048,128]{1,0:T(8,128)(2,1)} %param.14, bf16[192,2048]{1,0:T(8,128)(2,1)S(1)} %copy-done.2, f32[2048]{0:T(1024)S(1)} %copy-done.5, f32[192]{0:T(256)S(1)} %add_rsqrt_fusion), kind=kOutput, calls=%fused_computation.49 | convolution fusion | flops 102236160 | bytes 1417984 | tf_op jit(solution)/shard_map/dot_general | solution.py:508
  8.2 0.1 copy.28
  8.4 0.9 compare_and_fusion
  9.3 17.6 %shard_map.122 = bf16[5,192,256]{2,1,0:T(8,128)(2,1)S(1)} custom-call(bf16[192,256]{1,0:T(8,128)(2,1)S(1)} %pad_maximum_fusion.7.refs_0_), custom_call_target="tpu_custom_call" | custom-call | tf_op jit(solution)/shard_map/pallas_call | solution.py:97
  27.0 0.7 fusion.33
  27.7 1.8 %copy.29 = bf16[960,128]{0,1:T(8,128)(2,1)} copy(bf16[960,128]{1,0:T(8,128)(2,1)} %get-tuple-element.4) | data formatting | bytes 491520 | tf_op jit(solution)/shard_map/slice | solution.py:530
  29.5 0.9 copy.31
  30.4 2.6 %fusion.28 = f32[192,512]{0,1:T(8,128)S(1)} fusion(bf16[2048,512]{1,0:T(8,128)(2,1)} %param.13, bf16[192,2048]{1,0:T(8,128)(2,1)S(1)} %copy-done.2, f32[2048]{0:T(1024)S(1)} %copy-done.5, f32[192]{0:T(256)S(1)} %add_rsqrt_fusion), kind=kOutput, calls=%fused_computation.48 | convolution fusion | flops 404226048 | bytes 3285760 | tf_op jit(solution)/shard_map/dot_general | solution.py:507
  33.1 5.5 %fusion.34 = (f32[2,4,192]{2,1,0:T(4,128)S(1)}, bf16[2,4,192,960]{3,2,1,0:T(8,128)(2,1)}) fusion(pred[192,960]{1,0:T(8,128)(4,1)} %compare_and_fusion, bf16[960,2,64,1]{0,2,3,1:T(8,128)(2,1)S(1)} %bitcast.59, bf16[192,2,4,32]{0,3,2,1:T(8,128)(2,1)S(1)} %bitcast.63, bf16[192,2,4,32]{0,3,2,1:T(8,128)(2,1)S(1)} %bitcast.62), kind=kOutput, calls=%fused_computation.51 | convolution fusion | flops 197985216 | bytes 3581952 | tf_op jit(solution)/shard_map/sub | solution.py:539
  38.5 3.0 %fusion.16 = bf16[192,2,4,64]{0,3,2,1:T(8,128)(2,1)S(1)} fusion(bf16[960,2,64,1]{0,2,3,1:T(8,128)(2,1)S(1)} %bitcast.58, bf16[2,4,192,960]{3,2,1,0:T(8,128)(2,1)} %get-tuple-element.13, f32[192,2,4]{0,2,1:T(4,128)S(1)} %bitcast.67), kind=kOutput, calls=%fused_computation.17 | convolution fusion | flops 188940288 | bytes 3397632 | tf_op jit(solution)/shard_map/kgts,skd->kgtd/dot_general | solution.py:541
  41.6 0.6 convolution_convert_fusion
  42.2 9.6 %copy.33.refs_6_ = bf16[2048,1544]{1,0:T(8,128)(2,1)} copy(bf16[2048,1544]{0,1:T(8,128)(2,1)} %param.18) | data formatting | bytes 12648448 | tf_op args[7]
  51.8 52.7 %shard_map.123 = f32[4,8,384]{2,1,0:T(8,128)S(1)} custom-call(bf16[4,48,2048]{2,1,0:T(8,128)(2,1)S(1)} %bitcast.52, bf16[48,2048]{1,0:T(8,128)(2,1)S(1)} %constant_dynamic-slice_fusion.refs_1_, f32[1,2048]{1,0:T(1,128)S(1)} %bitcast.54, s32[4,1,384]{2,1,0:T(1,128)S(1)} %reshape.143.refs_3_, s32[1,1544]{1,0:T(1,128)S(1)} %broadcast_in_dim.70.refs_4_, ...), custom_call_target="tpu_custom_call" | custom-call | tf_op jit(solution)/shard_map/pallas_call | solution.py:376
  104.5 0.1 reshape.144
  104.6 0.1 reshape.145.refs_0_
  104.7 14.5 %shard_map.124 = f32[4,192]{1,0:T(4,128)S(1)} custom-call(f32[8,4,192]{2,1,0:T(4,128)S(1)} %reshape.145.refs_0_), custom_call_target="tpu_custom_call" | custom-call | tf_op jit(solution)/shard_map/pallas_call | solution.py:464
  119.2 0.6 divide_subtract_fusion
  (27 shorter events, 0.3 us)
Async XLA Ops:
  0.6 40.9 %copy-start = (bf16[512,2048]{1,0:T(8,128)(2,1)S(1)}, bf16[512,2048]{1,0:T(8,128)(2,1)}, u32[]{:S(2)}) copy-start(bf16[512,2048]{1,0:T(8,128)(2,1)} %param.16) | copy-start | bytes 6291460
  0.6 6.0 %copy-start.2 = (bf16[192,2048]{1,0:T(8,128)(2,1)S(1)}, bf16[192,2048]{1,0:T(8,128)(2,1)}, u32[]{:S(2)}) copy-start(bf16[192,2048]{1,0:T(8,128)(2,1)} %param.11) | copy-start | bytes 2359300
  0.7 6.0 %copy-start.5 = (f32[2048]{0:T(1024)S(1)}, f32[2048]{0:T(1024)}, u32[]{:S(2)}) copy-start(f32[2048]{0:T(1024)} %param.12) | copy-start | bytes 24580
  30.4 2.7 %copy-start.4 = (bf16[960,128]{0,1:T(8,128)(2,1)S(1)}, bf16[960,128]{0,1:T(8,128)(2,1)}, u32[]{:S(2)}) copy-start(bf16[960,128]{0,1:T(8,128)(2,1)} %copy.29) | copy-start | bytes 737284
  33.1 5.5 %copy-start.3 = (bf16[960,128]{0,1:T(8,128)(2,1)S(1)}, bf16[960,128]{0,1:T(8,128)(2,1)}, u32[]{:S(2)}) copy-start(bf16[960,128]{0,1:T(8,128)(2,1)} %copy.31) | copy-start | bytes 737284
  42.2 9.6 %copy-start.1 = (f32[2048]{0:T(1024)S(1)}, f32[2048]{0:T(1024)}, u32[]{:S(2)}) copy-start(f32[2048]{0:T(1024)} %param.17) | copy-start | bytes 24580

commit v4 on v3

--- a/solution.py
+++ b/solution.py
@@ -307,7 +307,7 @@
 
     depth = sizes["z"] * cores
     high = depth * rows
-    total_columns = head.shape[1]
+    total_columns = head.shape[0]
     cuts = [*range(0, total_columns - 511, 512)]
     tiles = list(zip(cuts, cuts[1:] + [total_columns])) if cuts else [(0, total_columns)]
 
@@ -319,7 +319,13 @@
         target = jnp.zeros((high, 1), jnp.float32)
         for low, end in tiles:
             logits = (
-                jnp.dot(block, head[:, low:end], preferred_element_type=jnp.float32) * LOGIT_SCALE
+                lax.dot_general(
+                    block,
+                    head[low:end, :],
+                    (((1,), (1,)), ((), ())),
+                    preferred_element_type=jnp.float32,
+                )
+                * LOGIT_SCALE
             )
             masked = jnp.where(live_ref[:, low:end] == 1, logits, NEG_FILL)
             scored[:, low:end] = masked
@@ -382,7 +388,7 @@
         scratch_shapes=[
             pltpu.VMEM((count, rows, width), jnp.bfloat16),
             pltpu.VMEM(head.shape, jnp.bfloat16),
-            pltpu.VMEM((high, head.shape[1]), jnp.float32),
+            pltpu.VMEM((high, head.shape[0]), jnp.float32),
             pltpu.VMEM((kv_size - 1, rows, width), jnp.bfloat16),
             pltpu.SemaphoreType.DMA,
             pltpu.SemaphoreType.DMA((kv_size - 1,)),
@@ -567,7 +573,7 @@
             target_ids,
             vocab_mask[None, :],
             columns[None, :],
-            w_head,
+            w_head.T,
             kv_size,
             seq_size,
         )

time: 120 us -> 107 us (0.89)
  local copies, waits for them, and re-layouts: 14.9 us -> 2.52 us
    unnamed x13 -> x14, local copies, waits for them, and re-layouts: 9.64 us -> 0.04 us
    slice x2, local copies, waits for them, and re-layouts: 2.51 us -> 0.88 us  [local(): key_rows = shard_rows[:, :key_width].reshape(row_count, kv_local, HEAD_DIM)]
where the time goes in v4:
time: 107 us; the launch traced here: 106 us
  Pallas kernels  85.5 us (80%)
  matrix products  13.9 us (13%)
  other arithmetic  3.56 us (3%)
  local copies, waits for them, and re-layouts  2.52 us (2%)
    pallas_call x1, Pallas kernels, score_rows(): pl.pallas_call(lambda *refs: head_kernel(kv_size, seq_size, *refs), out_s...  53.4 us
    pallas_call x1, Pallas kernels, gather_keys(): pl.pallas_call(lambda *refs: key_kernel(seq_size, reach, *refs), out_shap...  17.6 us
    pallas_call x1, Pallas kernels, merge_stats(): pl.pallas_call(lambda *refs: stat_kernel(kv_size, seq_size, *refs), out_s...  14.5 us
    sub x1, matrix products, local(): weights = jnp.where(allowed, jnp.exp(scores - top_score[..., None]), 0.0)  4.4 us
    dot_general x1, matrix products, local(): jnp.einsum('kgts,skd->kgtd', weights.astype(jnp.bfloat16), value_rows, pr...  3.01 us
    dot_general x1, matrix products, local(): queries = jnp.dot(normed_in, w_q, preferred_element_type=jnp.float32)  2.62 us

profile of v4, /device:TPU:0, one launch (start us, length us, event | category | flops | bytes accessed | tf_op | source)
XLA Modules:
  0.0 106.5 jit_solution(15740268498091034211)
XLA Ops:
  0.7 0.9 select_reduce_fusion.1
  1.6 0.1 select_reduce_fusion
  1.7 0.2 multiply_cosine_fusion
  1.9 1.4 %fusion.7 = f32[192]{0:T(256)S(1)} fusion(bf16[192,2048]{1,0:T(8,128)(2,1)} %param.11), kind=kLoop, calls=%fused_computation.12 | loop fusion | flops 1179456 | bytes 787200 | tf_op jit(solution)/shard_map/reduce_sum | solution.py:24
  3.3 1.8 %fusion.31 = f32[192,128]{0,1:T(8,128)S(1)} fusion(bf16[2048,128]{1,0:T(8,128)(2,1)} %param.14, bf16[192,2048]{1,0:T(8,128)(2,1)} %param.11, f32[2048]{0:T(1024)} %param.12, f32[192]{0:T(256)S(1)} %add_rsqrt_fusion), kind=kOutput, calls=%fused_computation.49 | convolution fusion | flops 102236160 | bytes 1417984 | tf_op jit(solution)/shard_map/dot_general | solution.py:514
  5.2 0.1 copy.26
  5.3 1.5 %convolution_convert_fusion.1 = bf16[192,128]{1,0:T(8,128)(2,1)S(1)} fusion(bf16[2048,128]{1,0:T(8,128)(2,1)} %param.15, bf16[192,2048]{1,0:T(8,128)(2,1)S(1)} %copy-done.2, f32[2048]{0:T(1024)S(1)} %copy-done.6, f32[192]{0:T(256)S(1)} %add_rsqrt_fusion), kind=kOutput, calls=%fused_computation.18 | convolution fusion | flops 102260736 | bytes 1368832 | tf_op jit(solution)/shard_map/dot_general | solution.py:515
  6.8 17.6 %shard_map.122 = bf16[5,192,256]{2,1,0:T(8,128)(2,1)S(1)} custom-call(bf16[192,256]{1,0:T(8,128)(2,1)S(1)} %pad_maximum_fusion.7.refs_0_), custom_call_target="tpu_custom_call" | custom-call | tf_op jit(solution)/shard_map/pallas_call | solution.py:97
  24.5 0.8 copy.27
  25.3 2.6 %fusion.28 = f32[192,512]{0,1:T(8,128)S(1)} fusion(bf16[2048,512]{1,0:T(8,128)(2,1)} %param.13, bf16[192,2048]{1,0:T(8,128)(2,1)S(1)} %copy-done.2, f32[2048]{0:T(1024)S(1)} %copy-done.6, f32[192]{0:T(256)S(1)} %add_rsqrt_fusion), kind=kOutput, calls=%fused_computation.48 | convolution fusion | flops 404226048 | bytes 3285760 | tf_op jit(solution)/shard_map/dot_general | solution.py:513
  28.0 0.1 subtract_convert_fusion
  28.0 0.2 compare_and_fusion
  28.3 4.4 %fusion.34 = (f32[2,4,192]{2,1,0:T(4,128)S(1)}, bf16[2,4,192,960]{3,2,1,0:T(8,128)(2,1)}) fusion(pred[192,960]{1,0:T(8,128)(4,1)S(1)} %compare_and_fusion, bf16[960,2,64,1]{0,2,3,1:T(8,128)(2,1)S(1)} %bitcast.60, bf16[192,2,4,32]{0,3,2,1:T(8,128)(2,1)S(1)} %bitcast.65, bf16[192,2,4,32]{0,3,2,1:T(8,128)(2,1)S(1)} %bitcast.64), kind=kOutput, calls=%fused_computation.51 | convolution fusion | flops 197985216 | bytes 3581952 | tf_op jit(solution)/shard_map/sub | solution.py:545
  32.7 0.1 copy.29
  32.8 3.0 %fusion.16 = bf16[192,2,4,64]{0,3,2,1:T(8,128)(2,1)S(1)} fusion(bf16[960,2,64,1]{0,2,3,1:T(8,128)(2,1)S(1)} %bitcast.61, bf16[2,4,192,960]{3,2,1,0:T(8,128)(2,1)} %get-tuple-element.13, f32[192,2,4]{0,2,1:T(4,128)S(1)} %bitcast.69), kind=kOutput, calls=%fused_computation.17 | convolution fusion | flops 188940288 | bytes 3397632 | tf_op jit(solution)/shard_map/kgts,skd->kgtd/dot_general | solution.py:547
  35.9 0.6 convolution_convert_fusion
  36.5 0.9 constant_dynamic-slice_fusion.refs_1_
  37.5 0.1 reshape.142
  37.6 0.1 reshape.143.refs_3_
  37.7 53.4 %shard_map.123 = f32[4,8,384]{2,1,0:T(8,128)S(1)} custom-call(bf16[4,48,2048]{2,1,0:T(8,128)(2,1)S(1)} %bitcast.53, bf16[48,2048]{1,0:T(8,128)(2,1)S(1)} %constant_dynamic-slice_fusion.refs_1_, f32[1,2048]{1,0:T(1,128)S(1)} %bitcast.55, s32[4,1,384]{2,1,0:T(1,128)S(1)} %reshape.143.refs_3_, s32[1,1544]{1,0:T(1,128)S(1)} %broadcast_in_dim.70.refs_4_, ...), custom_call_target="tpu_custom_call" | custom-call | tf_op jit(solution)/shard_map/pallas_call | solution.py:382
  91.1 0.1 reshape.144
  91.2 0.1 reshape.145.refs_0_
  91.3 14.5 %shard_map.124 = f32[4,192]{1,0:T(4,128)S(1)} custom-call(f32[8,4,192]{2,1,0:T(4,128)S(1)} %reshape.145.refs_0_), custom_call_target="tpu_custom_call" | custom-call | tf_op jit(solution)/shard_map/pallas_call | solution.py:470
  105.9 0.6 divide_subtract_fusion
  (28 shorter events, 0.2 us)
Async XLA Ops:
  0.6 35.3 %copy-start = (bf16[512,2048]{1,0:T(8,128)(2,1)S(1)}, bf16[512,2048]{1,0:T(8,128)(2,1)}, u32[]{:S(2)}) copy-start(bf16[512,2048]{1,0:T(8,128)(2,1)} %param.16) | copy-start | bytes 6291460
  0.6 4.6 %copy-start.2 = (bf16[192,2048]{1,0:T(8,128)(2,1)S(1)}, bf16[192,2048]{1,0:T(8,128)(2,1)}, u32[]{:S(2)}) copy-start(bf16[192,2048]{1,0:T(8,128)(2,1)} %param.11) | copy-start | bytes 2359300
  0.7 4.6 %copy-start.6 = (f32[2048]{0:T(1024)S(1)}, f32[2048]{0:T(1024)}, u32[]{:S(2)}) copy-start(f32[2048]{0:T(1024)} %param.12) | copy-start | bytes 24580
  25.3 3.0 %copy-start.3 = (bf16[960,128]{0,1:T(8,128)(2,1)S(1)}, bf16[960,128]{0,1:T(8,128)(2,1)}, u32[]{:S(2)}) copy-start(bf16[960,128]{0,1:T(8,128)(2,1)} %copy.27) | copy-start | bytes 737284
  35.9 1.6 %copy-start.4 = (s32[1536]{0:T(1024)S(1)}, s32[1536]{0:T(1024)}, u32[]{:S(2)}) copy-start(s32[1536]{0:T(1024)} %param.20) | copy-start | bytes 18436
  35.9 1.8 %copy-start.5 = (s32[1544]{0:T(1024)S(1)}, s32[1544]{0:T(1024)}, u32[]{:S(2)}) copy-start(s32[1544]{0:T(1024)} %param.21) | copy-start | bytes 18532
  35.9 1.8 %copy-start.1 = (f32[2048]{0:T(1024)S(1)}, f32[2048]{0:T(1024)}, u32[]{:S(2)}) copy-start(f32[2048]{0:T(1024)} %param.17) | copy-start | bytes 24580
